TPU v7x, 32 devices: a whole 2x2x4 slice. The times are simulated.
32 devices in a mesh: row: 4 (over y, x), col: 4 (over z), rep: 2 (over core).
Axes of the slice: x: 2, y: 2, z: 4, core: 2. Of those that a mesh axis runs over, the one named last changes fastest.
Arguments:
- features: bfloat16 [2, 2048, 512], P('rep', ('row', 'col')), may hold values from -6 to 6
- cotangent: bfloat16 [2, 2048, 512], P('rep', ('row', 'col')), may hold values from -6 to 6
- weight: bfloat16 [512, 512], replicated, may hold values from -0.25 to 0.25
- tile_values: bfloat16 [2, 256, 128, 128], P('rep', ('row', 'col')), may hold values from -0.25 to 0.25
- tile_out: int32 [2, 256], P('rep', ('row', 'col')), may hold values from 0 to 3
- tile_in: int32 [2, 256], P('rep', ('row', 'col')), may hold values from 0 to 3
- tile_count: int32 [2, 16], P('rep', ('row', 'col')), may hold values from 8 to 16, as said below
Outputs:
- out_feats: bfloat16 [2, 2048, 512], P('rep', ('row', 'col'))
- grad_feats: bfloat16 [2, 2048, 512], P('rep', ('row', 'col'))
- grad_weight: float32 [512, 512], replicated
Inputs may be any that keep to these rules, and one draw needn't show every extreme that they name: `tile_count`: in each window some group has all 16 slots live.
All inputs are finite; a program needn't handle non-finite values.
Results may differ from a plain program's by a relative error of at most 0.015.
Values may be sent and summed in bfloat16 or wider, within the bound.
A program may use at most 64 MiB of HBM per device.

v0:
```python
import jax
import jax.numpy as jnp
from jax import lax
from jax.sharding import PartitionSpec as P

SECTIONS = 4


def passed_along(value, axis, steps):
    count = lax.axis_size(axis)
    leading, last = (max(0, -steps), min(count, count - steps))
    return lax.ppermute(value, axis, [(source, source + steps) for source in range(leading, last)])


def body(features, cotangent, weight, tile_values, tile_out, tile_in, tile_count):
    field_in = features[0]
    values = tile_values[0]
    outs_idx = tile_out[0]
    ins_idx = tile_in[0]
    count = tile_count[0, 0]
    node_rows, width = field_in.shape
    edge = values.shape[-1]
    per_span = node_rows // edge
    half = SECTIONS // 2
    col_count = lax.axis_size("col")
    out_count = col_count * per_span
    in_count = SECTIONS * per_span
    slot_total = values.shape[0]
    live = (jnp.arange(slot_total, dtype=jnp.int32) < count).astype(jnp.float32)
    out_hot = (outs_idx[None, :] == jnp.arange(out_count, dtype=jnp.int32)[:, None]).astype(
        jnp.float32
    ) * live[None, :]
    in_hot = (ins_idx[None, :] == jnp.arange(in_count, dtype=jnp.int32)[:, None]).astype(
        jnp.float32
    ) * live[None, :]
    pieces = []
    for section in range(SECTIONS):
        offset = section - half
        if offset == 0:
            pieces.append(field_in)
        else:
            pieces.append(passed_along(field_in, "row", -offset))
    blocks = jnp.stack(pieces)
    picked = blocks[ins_idx]
    prods = jnp.einsum("tij,tjf->tif", values, picked, preferred_element_type=jnp.float32)
    part = jnp.einsum("ot,tif->oif", out_hot, prods, precision=lax.Precision.HIGHEST)
    summed = lax.psum_scatter(
        part.reshape(out_count * edge, width).astype(jnp.bfloat16),
        "col",
        scatter_dimension=0,
        tiled=True,
    )
    pre = jnp.dot(summed, weight, preferred_element_type=jnp.float32)
    out_feats = jax.nn.silu(pre).astype(jnp.bfloat16)
    sigma = jax.nn.sigmoid(pre)
    dpre = (cotangent[0].astype(jnp.float32) * sigma * (1.0 + pre * (1.0 - sigma))).astype(
        jnp.bfloat16
    )
    local_grad = jnp.einsum("nf,ng->fg", summed, dpre, preferred_element_type=jnp.float32)
    total_nodes = node_rows * lax.axis_size("row") * col_count * lax.axis_size("rep")
    grad_weight = lax.psum(local_grad, ("row", "col", "rep")) * jnp.float32(total_nodes) ** (-0.5)
    dhidden = jnp.einsum("nf,gf->ng", dpre, weight, preferred_element_type=jnp.float32).astype(
        jnp.bfloat16
    )
    row_grads = lax.all_gather(dhidden, "col", axis=0, tiled=True).reshape(out_count, edge, width)
    chosen = row_grads[outs_idx]
    back_prods = jnp.einsum("tij,tif->tjf", values, chosen, preferred_element_type=jnp.float32)
    sections_part = jnp.einsum("it,tjf->ijf", in_hot, back_prods, precision=lax.Precision.HIGHEST)
    sections_part = sections_part.astype(jnp.bfloat16)
    total = jnp.zeros((node_rows, width), jnp.float32)
    for section in range(SECTIONS):
        offset = section - half
        if offset == 0:
            arrived = sections_part[section]
        else:
            arrived = passed_along(sections_part[section], "row", offset)
        total = total + arrived.astype(jnp.float32)
    grad_feats = total.astype(jnp.bfloat16)
    return (out_feats[None], grad_feats[None], grad_weight)


def solution(mesh):
    return jax.shard_map(
        body,
        mesh=mesh,
        in_specs=(
            P("rep", ("row", "col"), None),
            P("rep", ("row", "col"), None),
            P(),
            P("rep", ("row", "col"), None, None),
            P("rep", ("row", "col")),
            P("rep", ("row", "col")),
            P("rep", ("row", "col")),
        ),
        out_specs=(P("rep", ("row", "col"), None), P("rep", ("row", "col"), None), P()),
        check_vma=False,
    )
```

profile of v0, /device:TPU:0, one launch (start us, length us, event | category | flops | bytes accessed | tf_op | source)
XLA Modules:
  0.0 224.5 jit_solution(10835809086337116893)
XLA Ops:
  7.2 5.0 %collective-permute-start = (bf16[128,512]{1,0:T(8,128)(2,1)}, bf16[128,512]{1,0:T(8,128)(2,1)S(1)}, u32[]{:S(2)}, u32[]{:S(2)}) collective-permute-start(bf16[128,512]{1,0:T(8,128)(2,1)} %bitcast.76), channel_id=1, source_target_pairs={{0,16},{8,24},{1,17},{9,25},{2,18},{10,26},{3,19},{11,27},{4,20},{... | collective-permute-start | bytes 393224 | tf_op jit(solution)/shard_map/ppermute | solution.py:12
  12.2 3.4 %collective-permute-start.1 = (bf16[128,512]{1,0:T(8,128)(2,1)}, bf16[128,512]{1,0:T(8,128)(2,1)S(1)}, u32[]{:S(2)}, u32[]{:S(2)}) collective-permute-start(bf16[128,512]{1,0:T(8,128)(2,1)} %bitcast.77), channel_id=1, source_target_pairs={{0,8},{8,16},{16,24},{1,9},{9,17},{17,25},{2,10},{10,18},{18,26},{... | collective-permute-start | bytes 393224 | tf_op jit(solution)/shard_map/ppermute | solution.py:12
  15.7 1.3 collective-permute-start.2
  18.5 4.3 %collective-permute-done.2 = bf16[128,512]{1,0:T(8,128)(2,1)S(1)} collective-permute-done((bf16[128,512]{1,0:T(8,128)(2,1)}, bf16[128,512]{1,0:T(8,128)(2,1)S(1)}, u32[]{:S(2)}, u32[]{:S(2)}) %collective-permute-start.2) | collective-permute-done | bytes 131104 | tf_op jit(solution)/shard_map/ppermute | solution.py:12
  22.7 1.0 pad_maximum_fusion
  24.4 2.7 %fusion.12 = f32[16,512,128]{2,1,0:T(8,128)} fusion(bf16[16,128,512]{2,1,0:T(8,128)(2,1)S(1)} %gather_fusion, bf16[1,16,128,128]{3,2,1,0:T(8,128)(2,1)S(1)} %copy-done), kind=kOutput, calls=%fused_computation.12 | convolution fusion | flops 268435456 | bytes 6815744 | tf_op jit(solution)/shard_map/tij,tjf->tif/dot_general | solution.py:45
  27.1 5.5 %copy.16 = f32[16,512,128]{1,0,2:T(8,128)} copy(f32[16,512,128]{2,1,0:T(8,128)} %fusion.12) | data formatting | bytes 8388608 | tf_op jit(solution)/shard_map/tij,tjf->tif/dot_general | solution.py:45
  32.6 4.3 %fusion.4 = bf16[4,128,512]{2,0,1:T(4,128)(2,1)S(1)} fusion(f32[16,512,128]{1,0,2:T(8,128)} %copy.16, f32[16]{0:T(128)S(1)} %compare_convert_fusion, s32[16]{0:T(128)S(1)} %bitcast.82), kind=kOutput, calls=%fused_computation.6 | convolution fusion | flops 50593920 | bytes 4718720 | tf_op jit(solution)/shard_map/ot,tif->oif/dot_general | solution.py:46
  37.0 0.9 copy.13
  38.0 21.4 %reduce-scatter.2.cloned.1.call-done = bf16[128,512]{1,0:T(8,128)(2,1)} async-done(((bf16[512,512]{1,0:T(8,128)(2,1)}), bf16[128,512]{1,0:T(8,128)(2,1)}) %reduce-scatter.2.cloned.1.call-update) | async-done | bytes 131088 | tf_op jit(solution)/shard_map/reduce_scatter | solution.py:47
  59.4 1.1 fusion.38
  60.9 15.9 %all_gather.3 = bf16[512,512]{1,0:T(8,128)(2,1)S(1)} all-gather(bf16[128,512]{1,0:T(8,128)(2,1)S(1)} %convolution_convert_fusion), channel_id=1, replica_groups=mesh['row'=4,'col'=4,'rep'=2] {'col'}, dimensions={0}, use_global_device_ids=true | all-gather | bytes 655360 | tf_op jit(solution)/shard_map/all_gather | solution.py:65
  77.4 2.8 %fusion.10 = f32[16,512,128]{2,1,0:T(8,128)} fusion(bf16[16,128,512]{2,1,0:T(8,128)(2,1)S(1)} %gather_fusion.1, bf16[1,16,128,128]{3,2,1,0:T(8,128)(2,1)S(1)} %copy-done), kind=kOutput, calls=%fused_computation.10 | convolution fusion | flops 268435456 | bytes 6815744 | tf_op jit(solution)/shard_map/tij,tif->tjf/dot_general | solution.py:67
  80.2 5.5 %copy.17 = f32[16,512,128]{1,0,2:T(8,128)} copy(f32[16,512,128]{2,1,0:T(8,128)} %fusion.10) | data formatting | bytes 8388608 | tf_op jit(solution)/shard_map/tij,tif->tjf/dot_general | solution.py:67
  85.7 1.4 fusion.34
  87.1 4.3 %fusion.7 = bf16[4,128,512]{2,0,1:T(4,128)(2,1)S(1)} fusion(f32[16,512,128]{1,0,2:T(8,128)} %copy.17, s32[16]{0:T(128)S(1)} %bitcast.83, f32[16]{0:T(128)S(1)} %compare_convert_fusion), kind=kOutput, calls=%fused_computation.7 | convolution fusion | flops 50593920 | bytes 4718720 | tf_op jit(solution)/shard_map/it,tjf->ijf/dot_general | solution.py:68
  91.4 0.7 fusion.37
  92.1 1.3 collective-permute-start.3
  93.5 1.3 collective-permute-start.4
  94.8 4.6 %collective-permute-start.5 = (bf16[128,512]{1,0:T(8,128)(2,1)S(1)}, bf16[128,512]{1,0:T(8,128)(2,1)S(1)}, u32[]{:S(2)}, u32[]{:S(2)}) collective-permute-start(bf16[128,512]{1,0:T(8,128)(2,1)S(1)} %bitcast.75), channel_id=1, source_target_pairs={{0,8},{8,16},{16,24},{1,9},{9,17},{17,25},{2,10},{10,18},{18,26},{... | collective-permute-start | bytes 393224 | tf_op jit(solution)/shard_map/ppermute | solution.py:12
  99.4 0.7 fusion.19
  100.3 1.7 collective-permute-done.5
  102.7 112.6 %all-reduce.2.cloned.1.call-done = f32[512,512]{1,0:T(8,128)} async-done(((f32[512,512]{1,0:T(8,128)}), f32[512,512]{1,0:T(8,128)}) %all-reduce.2.cloned.1.call-update) | async-done | bytes 1048592 | tf_op jit(solution)/shard_map/psum | solution.py:61
  215.3 2.3 %broadcast_multiply_fusion = f32[512,512]{1,0:T(8,128)} fusion(f32[512,512]{1,0:T(8,128)} %all-reduce.2.cloned.1.call-done), kind=kLoop, calls=%fused_computation.14 | loop fusion | flops 262144 | bytes 2097152 | tf_op jit(solution)/shard_map/mul | solution.py:61
  (32 shorter events, 3.7 us)
Async XLA Ops:
  7.2 17.2 %copy-start = (bf16[1,16,128,128]{3,2,1,0:T(8,128)(2,1)S(1)}, bf16[1,16,128,128]{3,2,1,0:T(8,128)(2,1)}, u32[]{:S(2)}) copy-start(bf16[1,16,128,128]{3,2,1,0:T(8,128)(2,1)} %param.10) | copy-start | bytes 1572868
  7.2 52.2 %reduce-scatter.2.cloned.1.call-start = ((), (), s32[]{:S(2)}) async-start(), calls=%async_computation.1 | async-start | bytes 655360 | tf_op jit(solution)/shard_map/reduce_scatter | solution.py:47
  7.2 11.1 %collective-permute-start = (bf16[128,512]{1,0:T(8,128)(2,1)}, bf16[128,512]{1,0:T(8,128)(2,1)S(1)}, u32[]{:S(2)}, u32[]{:S(2)}) collective-permute-start(bf16[128,512]{1,0:T(8,128)(2,1)} %bitcast.76), channel_id=1, source_target_pairs={{0,16},{8,24},{1,17},{9,25},{2,18},{10,26},{3,19},{11,27},{4,20},{... | collective-permute-start | bytes 393224 | tf_op jit(solution)/shard_map/ppermute | solution.py:12
  12.2 6.2 %collective-permute-start.1 = (bf16[128,512]{1,0:T(8,128)(2,1)}, bf16[128,512]{1,0:T(8,128)(2,1)S(1)}, u32[]{:S(2)}, u32[]{:S(2)}) collective-permute-start(bf16[128,512]{1,0:T(8,128)(2,1)} %bitcast.77), channel_id=1, source_target_pairs={{0,8},{8,16},{16,24},{1,9},{9,17},{17,25},{2,10},{10,18},{18,26},{... | collective-permute-start | bytes 393224 | tf_op jit(solution)/shard_map/ppermute | solution.py:12
  15.7 7.1 %collective-permute-start.2 = (bf16[128,512]{1,0:T(8,128)(2,1)}, bf16[128,512]{1,0:T(8,128)(2,1)S(1)}, u32[]{:S(2)}, u32[]{:S(2)}) collective-permute-start(bf16[128,512]{1,0:T(8,128)(2,1)} %bitcast.78), channel_id=1, source_target_pairs={{8,0},{16,8},{24,16},{9,1},{17,9},{25,17},{10,2},{18,10},{26,18},{... | collective-permute-start | bytes 393224 | tf_op jit(solution)/shard_map/ppermute | solution.py:12
  27.1 5.5 %copy-start.3 = (s32[1,16]{1,0:T(1,128)S(1)}, s32[1,16]{1,0:T(1,128)}, u32[]{:S(2)}) copy-start(s32[1,16]{1,0:T(1,128)} %param.11) | copy-start | bytes 196
  32.6 26.8 %copy-start.1 = (bf16[512,512]{1,0:T(8,128)(2,1)S(1)}, bf16[512,512]{1,0:T(8,128)(2,1)}, u32[]{:S(2)}) copy-start(bf16[512,512]{1,0:T(8,128)(2,1)} %param.9) | copy-start | bytes 1572868
  37.0 23.6 %copy-start.5 = (bf16[1,128,512]{2,1,0:T(8,128)(2,1)S(1)}, bf16[1,128,512]{2,1,0:T(8,128)(2,1)}, u32[]{:S(2)}) copy-start(bf16[1,128,512]{2,1,0:T(8,128)(2,1)} %param.8) | copy-start | bytes 393220
  37.9 177.4 %all-reduce.2.cloned.1.call-start = ((), (), s32[]{:S(2)}) async-start(), calls=%async_computation.2 | async-start | bytes 2097152 | tf_op jit(solution)/shard_map/psum | solution.py:61
  80.2 5.5 %copy-start.2 = (bf16[128,512]{1,0:T(8,128)(2,1)S(1)}, bf16[128,512]{1,0:T(8,128)(2,1)}, u32[]{:S(2)}) copy-start(bf16[128,512]{1,0:T(8,128)(2,1)} %reduce-scatter.2.cloned.1.call-done) | copy-start | bytes 393220
  85.7 1.4 copy-start.4
  92.1 8.0 %collective-permute-start.3 = (bf16[128,512]{1,0:T(8,128)(2,1)S(1)}, bf16[128,512]{1,0:T(8,128)(2,1)S(1)}, u32[]{:S(2)}, u32[]{:S(2)}) collective-permute-start(bf16[128,512]{1,0:T(8,128)(2,1)S(1)} %bitcast.73), channel_id=1, source_target_pairs={{16,0},{24,8},{17,1},{25,9},{18,2},{26,10},{19,3},{27,11},{20,4},{... | collective-permute-start | bytes 393224 | tf_op jit(solution)/shard_map/ppermute | solution.py:12
  93.5 6.9 %collective-permute-start.4 = (bf16[128,512]{1,0:T(8,128)(2,1)S(1)}, bf16[128,512]{1,0:T(8,128)(2,1)S(1)}, u32[]{:S(2)}, u32[]{:S(2)}) collective-permute-start(bf16[128,512]{1,0:T(8,128)(2,1)S(1)} %bitcast.74), channel_id=1, source_target_pairs={{8,0},{16,8},{24,16},{9,1},{17,9},{25,17},{10,2},{18,10},{26,18},{... | collective-permute-start | bytes 393224 | tf_op jit(solution)/shard_map/ppermute | solution.py:12
  94.8 7.2 %collective-permute-start.5 = (bf16[128,512]{1,0:T(8,128)(2,1)S(1)}, bf16[128,512]{1,0:T(8,128)(2,1)S(1)}, u32[]{:S(2)}, u32[]{:S(2)}) collective-permute-start(bf16[128,512]{1,0:T(8,128)(2,1)S(1)} %bitcast.75), channel_id=1, source_target_pairs={{0,8},{8,16},{16,24},{1,9},{9,17},{17,25},{2,10},{10,18},{18,26},{... | collective-permute-start | bytes 393224 | tf_op jit(solution)/shard_map/ppermute | solution.py:12
Sparse Core Ops, SparseCore 0:
  38.0 21.3 reduce-scatter.1
  87.2 128.0 all-reduce.1
where the time goes:
time: 225 us; the launch traced here: 224 us
  waiting for transfers between devices  140 us (62%)
  starting transfers between devices  16.9 us (8%)
  matrix products  16.9 us (8%)
  blocking collectives  15.9 us (7%)
  between operations  14.9 us (7%)
  local copies, waits for them, and re-layouts  13.4 us (6%)
  other arithmetic  6.11 us (3%)
    psum x1, waiting for transfers between devices, body(): lax.psum(local_grad, ('row', 'col', 'rep'))  113 us
    reduce_scatter x1, waiting for transfers between devices, body(): lax.psum_scatter(part.reshape(out_count * edge, width).astype(jnp.bfloat1...  21.4 us
    ppermute x6, starting transfers between devices, passed_along(): lax.ppermute(value, axis, [(source, source + steps) for source in range(l...  16.8 us
    all_gather x1, blocking collectives, body(): lax.all_gather(dhidden, 'col', axis=0, tiled=True)  15.9 us
    ppermute x6, waiting for transfers between devices, passed_along(): lax.ppermute(value, axis, [(source, source + steps) for source in range(l...  6.33 us
    dot_general x1, local copies, waits for them, and re-layouts, body(): jnp.einsum('tij,tif->tjf', values, chosen, preferred_element_type=jnp.flo...  5.54 us
    dot_general x1, local copies, waits for them, and re-layouts, body(): jnp.einsum('tij,tjf->tif', values, picked, preferred_element_type=jnp.flo...  5.51 us
  transfers between devices with their start and end apart: 8, of which 6 were waited for; matrix products, arithmetic and copies ran while one was open for 3% of the time, Pallas kernels for 0%

commit v1 on v0

--- a/solution.py
+++ b/solution.py
@@ -4,6 +4,22 @@
 from jax.sharding import PartitionSpec as P
 
 SECTIONS = 4
+
+
+def ring_gather(x, axis, dim):
+    ways, here, step = (lax.axis_size(axis), lax.axis_index(axis), x.shape[dim])
+    dims = [n * ways if d == dim else n for d, n in enumerate(x.shape)]
+    full = lax.dynamic_update_slice_in_dim(jnp.zeros(dims, x.dtype), x, here * step, axis=dim)
+    going_up = going_down = x
+    for far in range(1, ways // 2 + 1):
+        going_up = lax.ppermute(going_up, axis, [(d, (d + 1) % ways) for d in range(ways)])
+        full = lax.dynamic_update_slice_in_dim(full, going_up, (here - far) % ways * step, axis=dim)
+        if 2 * far < ways:
+            going_down = lax.ppermute(going_down, axis, [(d, (d - 1) % ways) for d in range(ways)])
+            full = lax.dynamic_update_slice_in_dim(
+                full, going_down, (here + far) % ways * step, axis=dim
+            )
+    return full
 
 
 def passed_along(value, axis, steps):
@@ -62,7 +78,7 @@
     dhidden = jnp.einsum("nf,gf->ng", dpre, weight, preferred_element_type=jnp.float32).astype(
         jnp.bfloat16
     )
-    row_grads = lax.all_gather(dhidden, "col", axis=0, tiled=True).reshape(out_count, edge, width)
+    row_grads = ring_gather(dhidden, "col", 0).reshape(out_count, edge, width)
     chosen = row_grads[outs_idx]
     back_prods = jnp.einsum("tij,tif->tjf", values, chosen, preferred_element_type=jnp.float32)
     sections_part = jnp.einsum("it,tjf->ijf", in_hot, back_prods, precision=lax.Precision.HIGHEST)

time: 225 us -> 204 us (0.907)
  blocking collectives: 15.9 us -> 0 us
  waiting for transfers between devices: 140 us -> 132 us
  starting transfers between devices: 16.9 us -> 20.8 us
    psum x1, waiting for transfers between devices: 113 us -> 94.2 us  [body(): lax.psum(local_grad, ('row', 'col', 'rep'))]
    all_gather x1 -> x0, blocking collectives: 15.9 us -> none  [body(): lax.all_gather(dhidden, 'col', axis=0, tiled=True)]
    ppermute x0 -> x3, waiting for transfers between devices: none -> 9.13 us  [the longest x2 9.13 us: ring_gather(): lax.ppermute(going_up, axis, [(d, (d + 1) % ways) for d in range(ways)])]
    ppermute x0 -> x3, starting transfers between devices: none -> 3.87 us  [the longest x1 3.81 us: ring_gather(): lax.ppermute(going_down, axis, [(d, (d - 1) % ways) for d in range(ways)])]
  transfers between devices with their start and end apart: 8 -> 11, of which waited for: 6 -> 8; matrix products, arithmetic and copies ran while one was open for 3% -> 9% of each run, Pallas kernels for 0% -> 0%
where the time goes in v1:
time: 204 us
  waiting for transfers between devices  132 us (65%)
  starting transfers between devices  20.8 us (10%)
  matrix products  17 us (8%)
  between operations  15 us (7%)
  local copies, waits for them, and re-layouts  13.5 us (7%)
  other arithmetic  6.11 us (3%)
    psum x1, waiting for transfers between devices, body(): lax.psum(local_grad, ('row', 'col', 'rep'))  94.2 us
    reduce_scatter x1, waiting for transfers between devices, body(): lax.psum_scatter(part.reshape(out_count * edge, width).astype(jnp.bfloat1...  21.4 us
    ppermute x6, starting transfers between devices, passed_along(): lax.ppermute(value, axis, [(source, source + steps) for source in range(l...  16.8 us
    ppermute x2, waiting for transfers between devices, ring_gather(): lax.ppermute(going_up, axis, [(d, (d + 1) % ways) for d in range(ways)])  9.13 us
    ppermute x6, waiting for transfers between devices, passed_along(): lax.ppermute(value, axis, [(source, source + steps) for source in range(l...  6.86 us
    dot_general x1, local copies, waits for them, and re-layouts, body(): jnp.einsum('tij,tif->tjf', values, chosen, preferred_element_type=jnp.flo...  5.52 us
    dot_general x1, local copies, waits for them, and re-layouts, body(): jnp.einsum('tij,tjf->tif', values, picked, preferred_element_type=jnp.flo...  5.51 us
    dot_general x1, matrix products, body(): jnp.einsum('ot,tif->oif', out_hot, prods, precision=lax.Precision.HIGHEST)  4.33 us
  transfers between devices with their start and end apart: 11, of which 8 were waited for; matrix products, arithmetic and copies ran while one was open for 9% of the time, Pallas kernels for 0%

profile of v1, /device:TPU:0, one launch (start us, length us, event | category | flops | bytes accessed | tf_op | source)
XLA Modules:
  0.0 203.9 jit_solution(7871122721037286208)
XLA Ops:
  7.2 5.0 %collective-permute-start = (bf16[128,512]{1,0:T(8,128)(2,1)}, bf16[128,512]{1,0:T(8,128)(2,1)S(1)}, u32[]{:S(2)}, u32[]{:S(2)}) collective-permute-start(bf16[128,512]{1,0:T(8,128)(2,1)} %bitcast.78), channel_id=1, source_target_pairs={{0,16},{8,24},{1,17},{9,25},{2,18},{10,26},{3,19},{11,27},{4,20},{... | collective-permute-start | bytes 393224 | tf_op jit(solution)/shard_map/ppermute | solution.py:28
  12.2 3.4 %collective-permute-start.1 = (bf16[128,512]{1,0:T(8,128)(2,1)}, bf16[128,512]{1,0:T(8,128)(2,1)S(1)}, u32[]{:S(2)}, u32[]{:S(2)}) collective-permute-start(bf16[128,512]{1,0:T(8,128)(2,1)} %bitcast.79), channel_id=1, source_target_pairs={{0,8},{8,16},{16,24},{1,9},{9,17},{17,25},{2,10},{10,18},{18,26},{... | collective-permute-start | bytes 393224 | tf_op jit(solution)/shard_map/ppermute | solution.py:28
  15.7 1.3 collective-permute-start.2
  18.5 4.3 %collective-permute-done.2 = bf16[128,512]{1,0:T(8,128)(2,1)S(1)} collective-permute-done((bf16[128,512]{1,0:T(8,128)(2,1)}, bf16[128,512]{1,0:T(8,128)(2,1)S(1)}, u32[]{:S(2)}, u32[]{:S(2)}) %collective-permute-start.2) | collective-permute-done | bytes 131104 | tf_op jit(solution)/shard_map/ppermute | solution.py:28
  22.7 1.0 pad_maximum_fusion
  24.4 2.7 %fusion.12 = f32[16,512,128]{2,1,0:T(8,128)} fusion(bf16[16,128,512]{2,1,0:T(8,128)(2,1)S(1)} %gather_fusion, bf16[1,16,128,128]{3,2,1,0:T(8,128)(2,1)S(1)} %copy-done), kind=kOutput, calls=%fused_computation.12 | convolution fusion | flops 268435456 | bytes 6815744 | tf_op jit(solution)/shard_map/tij,tjf->tif/dot_general | solution.py:61
  27.1 5.5 %copy.16 = f32[16,512,128]{1,0,2:T(8,128)} copy(f32[16,512,128]{2,1,0:T(8,128)} %fusion.12) | data formatting | bytes 8388608 | tf_op jit(solution)/shard_map/tij,tjf->tif/dot_general | solution.py:61
  32.7 4.3 %fusion.4 = bf16[4,128,512]{2,0,1:T(4,128)(2,1)S(1)} fusion(f32[16,512,128]{1,0,2:T(8,128)} %copy.16, f32[16]{0:T(128)S(1)} %compare_convert_fusion, s32[16]{0:T(128)S(1)} %bitcast.84), kind=kOutput, calls=%fused_computation.6 | convolution fusion | flops 50593920 | bytes 4718720 | tf_op jit(solution)/shard_map/ot,tif->oif/dot_general | solution.py:62
  37.0 0.9 copy.13
  38.1 21.4 %reduce-scatter.2.cloned.1.call-done = bf16[128,512]{1,0:T(8,128)(2,1)} async-done(((bf16[512,512]{1,0:T(8,128)(2,1)}), bf16[128,512]{1,0:T(8,128)(2,1)}) %reduce-scatter.2.cloned.1.call-update) | async-done | bytes 131088 | tf_op jit(solution)/shard_map/reduce_scatter | solution.py:63
  59.5 1.2 fusion.38
  61.1 3.8 %collective-permute-start.4 = (bf16[128,512]{1,0:T(8,128)(2,1)S(1)}, bf16[128,512]{1,0:T(8,128)(2,1)S(1)}, u32[]{:S(2)}, u32[]{:S(2)}) collective-permute-start(bf16[128,512]{1,0:T(8,128)(2,1)S(1)} %get-tuple-element.8), channel_id=1, source_target_pairs={{0,6},{2,0},{4,2},{6,4},{1,7},{3,1},{5,3},{7,5},{8,14},{10,8},{12,... | collective-permute-start | bytes 393224 | tf_op jit(solution)/shard_map/ppermute | solution.py:18
  64.9 1.3 fusion.34
  66.3 1.7 collective-permute-done.3
  68.0 7.5 %collective-permute-done.5 = bf16[128,512]{1,0:T(8,128)(2,1)S(1)} collective-permute-done((bf16[128,512]{1,0:T(8,128)(2,1)S(1)}, bf16[128,512]{1,0:T(8,128)(2,1)S(1)}, u32[]{:S(2)}, u32[]{:S(2)}) %collective-permute-start.5) | collective-permute-done | bytes 131104 | tf_op jit(solution)/shard_map/ppermute | solution.py:15
  76.2 2.7 %fusion.10 = f32[16,512,128]{2,1,0:T(8,128)} fusion(bf16[16,128,512]{2,1,0:T(8,128)(2,1)S(1)} %gather_fusion.1, bf16[1,16,128,128]{3,2,1,0:T(8,128)(2,1)S(1)} %copy-done), kind=kOutput, calls=%fused_computation.10 | convolution fusion | flops 268435456 | bytes 6815744 | tf_op jit(solution)/shard_map/tij,tif->tjf/dot_general | solution.py:83
  78.9 5.5 %copy.17 = f32[16,512,128]{1,0,2:T(8,128)} copy(f32[16,512,128]{2,1,0:T(8,128)} %fusion.10) | data formatting | bytes 8388608 | tf_op jit(solution)/shard_map/tij,tif->tjf/dot_general | solution.py:83
  84.4 4.3 %fusion.7 = bf16[4,128,512]{2,0,1:T(4,128)(2,1)S(1)} fusion(f32[16,512,128]{1,0,2:T(8,128)} %copy.17, s32[16]{0:T(128)S(1)} %bitcast.85, f32[16]{0:T(128)S(1)} %compare_convert_fusion), kind=kOutput, calls=%fused_computation.7 | convolution fusion | flops 50593920 | bytes 4718720 | tf_op jit(solution)/shard_map/it,tjf->ijf/dot_general | solution.py:84
  89.5 1.3 collective-permute-start.6
  90.8 1.3 collective-permute-start.7
  92.2 4.6 %collective-permute-start.8 = (bf16[128,512]{1,0:T(8,128)(2,1)S(1)}, bf16[128,512]{1,0:T(8,128)(2,1)S(1)}, u32[]{:S(2)}, u32[]{:S(2)}) collective-permute-start(bf16[128,512]{1,0:T(8,128)(2,1)S(1)} %bitcast.77), channel_id=1, source_target_pairs={{0,8},{8,16},{16,24},{1,9},{9,17},{17,25},{2,10},{10,18},{18,26},{... | collective-permute-start | bytes 393224 | tf_op jit(solution)/shard_map/ppermute | solution.py:28
  97.7 2.2 %collective-permute-done.8 = bf16[128,512]{1,0:T(8,128)(2,1)S(1)} collective-permute-done((bf16[128,512]{1,0:T(8,128)(2,1)S(1)}, bf16[128,512]{1,0:T(8,128)(2,1)S(1)}, u32[]{:S(2)}, u32[]{:S(2)}) %collective-permute-start.8) | collective-permute-done | bytes 131104 | tf_op jit(solution)/shard_map/ppermute | solution.py:28
  100.6 94.2 %all-reduce.2.cloned.1.call-done = f32[512,512]{1,0:T(8,128)} async-done(((f32[512,512]{1,0:T(8,128)}), f32[512,512]{1,0:T(8,128)}) %all-reduce.2.cloned.1.call-update) | async-done | bytes 1048592 | tf_op jit(solution)/shard_map/psum | solution.py:77
  194.8 2.3 %broadcast_multiply_fusion = f32[512,512]{1,0:T(8,128)} fusion(f32[512,512]{1,0:T(8,128)} %all-reduce.2.cloned.1.call-done), kind=kLoop, calls=%fused_computation.14 | loop fusion | flops 262144 | bytes 2097152 | tf_op jit(solution)/shard_map/mul | solution.py:77
  (41 shorter events, 5.3 us)
Async XLA Ops:
  7.2 17.2 %copy-start = (bf16[1,16,128,128]{3,2,1,0:T(8,128)(2,1)S(1)}, bf16[1,16,128,128]{3,2,1,0:T(8,128)(2,1)}, u32[]{:S(2)}) copy-start(bf16[1,16,128,128]{3,2,1,0:T(8,128)(2,1)} %param.10) | copy-start | bytes 1572868
  7.2 52.3 %reduce-scatter.2.cloned.1.call-start = ((), (), s32[]{:S(2)}) async-start(), calls=%async_computation.1 | async-start | bytes 655360 | tf_op jit(solution)/shard_map/reduce_scatter | solution.py:63
  7.2 11.1 %collective-permute-start = (bf16[128,512]{1,0:T(8,128)(2,1)}, bf16[128,512]{1,0:T(8,128)(2,1)S(1)}, u32[]{:S(2)}, u32[]{:S(2)}) collective-permute-start(bf16[128,512]{1,0:T(8,128)(2,1)} %bitcast.78), channel_id=1, source_target_pairs={{0,16},{8,24},{1,17},{9,25},{2,18},{10,26},{3,19},{11,27},{4,20},{... | collective-permute-start | bytes 393224 | tf_op jit(solution)/shard_map/ppermute | solution.py:28
  12.2 6.2 %collective-permute-start.1 = (bf16[128,512]{1,0:T(8,128)(2,1)}, bf16[128,512]{1,0:T(8,128)(2,1)S(1)}, u32[]{:S(2)}, u32[]{:S(2)}) collective-permute-start(bf16[128,512]{1,0:T(8,128)(2,1)} %bitcast.79), channel_id=1, source_target_pairs={{0,8},{8,16},{16,24},{1,9},{9,17},{17,25},{2,10},{10,18},{18,26},{... | collective-permute-start | bytes 393224 | tf_op jit(solution)/shard_map/ppermute | solution.py:28
  15.7 7.1 %collective-permute-start.2 = (bf16[128,512]{1,0:T(8,128)(2,1)}, bf16[128,512]{1,0:T(8,128)(2,1)S(1)}, u32[]{:S(2)}, u32[]{:S(2)}) collective-permute-start(bf16[128,512]{1,0:T(8,128)(2,1)} %bitcast.80), channel_id=1, source_target_pairs={{8,0},{16,8},{24,16},{9,1},{17,9},{25,17},{10,2},{18,10},{26,18},{... | collective-permute-start | bytes 393224 | tf_op jit(solution)/shard_map/ppermute | solution.py:28
  27.1 5.5 %copy-start.3 = (s32[1,16]{1,0:T(1,128)S(1)}, s32[1,16]{1,0:T(1,128)}, u32[]{:S(2)}) copy-start(s32[1,16]{1,0:T(1,128)} %param.11) | copy-start | bytes 196
  32.7 26.8 %copy-start.1 = (bf16[512,512]{1,0:T(8,128)(2,1)S(1)}, bf16[512,512]{1,0:T(8,128)(2,1)}, u32[]{:S(2)}) copy-start(bf16[512,512]{1,0:T(8,128)(2,1)} %param.9) | copy-start | bytes 1572868
  37.0 23.7 %copy-start.5 = (bf16[1,128,512]{2,1,0:T(8,128)(2,1)S(1)}, bf16[1,128,512]{2,1,0:T(8,128)(2,1)}, u32[]{:S(2)}) copy-start(bf16[1,128,512]{2,1,0:T(8,128)(2,1)} %param.8) | copy-start | bytes 393220
  37.9 156.9 %all-reduce.2.cloned.1.call-start = ((), (), s32[]{:S(2)}) async-start(), calls=%async_computation.2 | async-start | bytes 2097152 | tf_op jit(solution)/shard_map/psum | solution.py:77
  59.4 5.5 %copy-start.2 = (bf16[128,512]{1,0:T(8,128)(2,1)S(1)}, bf16[128,512]{1,0:T(8,128)(2,1)}, u32[]{:S(2)}) copy-start(bf16[128,512]{1,0:T(8,128)(2,1)} %reduce-scatter.2.cloned.1.call-done) | copy-start | bytes 393220
  61.0 6.9 %collective-permute-start.3 = (bf16[128,512]{1,0:T(8,128)(2,1)S(1)}, bf16[128,512]{1,0:T(8,128)(2,1)S(1)}, u32[]{:S(2)}, u32[]{:S(2)}) collective-permute-start(bf16[128,512]{1,0:T(8,128)(2,1)S(1)} %get-tuple-element.8), channel_id=1, source_target_pairs={{0,2},{2,4},{4,6},{6,0},{1,3},{3,5},{5,7},{7,1},{8,10},{10,12},{12... | collective-permute-start | bytes 393224 | tf_op jit(solution)/shard_map/ppermute | solution.py:15
  61.1 6.9 %collective-permute-start.4 = (bf16[128,512]{1,0:T(8,128)(2,1)S(1)}, bf16[128,512]{1,0:T(8,128)(2,1)S(1)}, u32[]{:S(2)}, u32[]{:S(2)}) collective-permute-start(bf16[128,512]{1,0:T(8,128)(2,1)S(1)} %get-tuple-element.8), channel_id=1, source_target_pairs={{0,6},{2,0},{4,2},{6,4},{1,7},{3,1},{5,3},{7,5},{8,14},{10,8},{12,... | collective-permute-start | bytes 393224 | tf_op jit(solution)/shard_map/ppermute | solution.py:18
  68.0 7.5 %collective-permute-start.5 = (bf16[128,512]{1,0:T(8,128)(2,1)S(1)}, bf16[128,512]{1,0:T(8,128)(2,1)S(1)}, u32[]{:S(2)}, u32[]{:S(2)}) collective-permute-start(bf16[128,512]{1,0:T(8,128)(2,1)S(1)} %collective-permute-done.3), channel_id=1, source_target_pairs={{0,2},{2,4},{4,6},{6,0},{1,3},{3,5},{5,7},{7,1},{8,10},{10,12},{12... | collective-permute-start | bytes 393224 | tf_op jit(solution)/shard_map/ppermute | solution.py:15
  78.9 5.5 %copy-start.4 = (s32[1,16]{1,0:T(1,128)S(1)}, s32[1,16]{1,0:T(1,128)}, u32[]{:S(2)}) copy-start(s32[1,16]{1,0:T(1,128)} %param.12) | copy-start | bytes 196
  89.5 8.0 %collective-permute-start.6 = (bf16[128,512]{1,0:T(8,128)(2,1)S(1)}, bf16[128,512]{1,0:T(8,128)(2,1)S(1)}, u32[]{:S(2)}, u32[]{:S(2)}) collective-permute-start(bf16[128,512]{1,0:T(8,128)(2,1)S(1)} %bitcast.75), channel_id=1, source_target_pairs={{16,0},{24,8},{17,1},{25,9},{18,2},{26,10},{19,3},{27,11},{20,4},{... | collective-permute-start | bytes 393224 | tf_op jit(solution)/shard_map/ppermute | solution.py:28
  90.8 6.9 %collective-permute-start.7 = (bf16[128,512]{1,0:T(8,128)(2,1)S(1)}, bf16[128,512]{1,0:T(8,128)(2,1)S(1)}, u32[]{:S(2)}, u32[]{:S(2)}) collective-permute-start(bf16[128,512]{1,0:T(8,128)(2,1)S(1)} %bitcast.76), channel_id=1, source_target_pairs={{8,0},{16,8},{24,16},{9,1},{17,9},{25,17},{10,2},{18,10},{26,18},{... | collective-permute-start | bytes 393224 | tf_op jit(solution)/shard_map/ppermute | solution.py:28
  92.2 7.7 %collective-permute-start.8 = (bf16[128,512]{1,0:T(8,128)(2,1)S(1)}, bf16[128,512]{1,0:T(8,128)(2,1)S(1)}, u32[]{:S(2)}, u32[]{:S(2)}) collective-permute-start(bf16[128,512]{1,0:T(8,128)(2,1)S(1)} %bitcast.77), channel_id=1, source_target_pairs={{0,8},{8,16},{16,24},{1,9},{9,17},{17,25},{2,10},{10,18},{18,26},{... | collective-permute-start | bytes 393224 | tf_op jit(solution)/shard_map/ppermute | solution.py:28
Sparse Core Ops, SparseCore 0:
  38.0 21.3 reduce-scatter.1
  66.4 128.3 all-reduce.1
